TPU v7x, 512 devices: a whole 4x8x8 slice. The times are simulated.
512 devices in a mesh: seq: 32 (over y, x), head: 2 (over core), expert: 8 (over z).
Axes of the slice: x: 4, y: 8, z: 8, core: 2. Of those that a mesh axis runs over, the one named last changes fastest.
Arguments:
- query_proj: bfloat16 [8, 4096, 2048], P('expert', 'seq', 'head'), may hold values from -6 to 6
- key_proj: bfloat16 [8, 4096, 2048], P('expert', 'seq', 'head'), may hold values from -6 to 6
- value_proj: bfloat16 [8, 4096, 2048], P('expert', 'seq', 'head'), may hold values from -6 to 6
- init_state: float32 [8, 16, 128, 128], P('expert', 'head'), may hold values from -384 to 384
- residual: bfloat16 [8, 4096, 2048], P('expert', ('seq', 'head')), may hold values from -6 to 6
- out_gain: float32 [2048], P('head'), may hold values from 0.1 to 1.9
- proj_weight: bfloat16 [2048, 2048], P('head', 'expert'), may hold values from -0.125 to 0.125
- moe_gain: float32 [2048], replicated, may hold values from 0.1 to 1.9
- w_gate: bfloat16 [64, 704, 2048], P(('seq', 'head'), None, 'expert'), may hold values from -0.125 to 0.125
- w_up: bfloat16 [64, 704, 2048], P(('seq', 'head'), None, 'expert'), may hold values from -0.125 to 0.125
- w_down: bfloat16 [64, 704, 2048], P(('seq', 'head'), None, 'expert'), may hold values from -0.21875 to 0.21875
- expert_ids: int32 [8, 4096, 6], P('expert', ('seq', 'head')), may hold values from 0 to 63, all different within a row; in each aligned block of 64 rows (0 to 63, 64 to 127, ..., all dimensions but the last counted through in order) at most 8 rows name the same one
- gate_weights: float32 [8, 4096, 6], P('expert', ('seq', 'head')), may hold values from 0.05 to 0.5
Outputs:
- layer_out: bfloat16 [8, 4096, 2048], P('expert', ('seq', 'head'))
Inputs may be any that keep to these rules, and one draw needn't show every extreme that they name: `expert_ids`: each token names 6 different experts. Among the 64 tokens of one device (aligned blocks of 64 positions) no expert is named more than 8 times, a bound that some block reaches.
All inputs are finite; a program needn't handle non-finite values.
Results may differ from a plain program's by a relative error of at most 0.019.
Values may be sent and summed in bfloat16 or wider, within the bound.
A program may use at most 128 MiB of HBM per device.

v0:
```python
import jax
import jax.numpy as jnp
from jax import lax
from jax.sharding import PartitionSpec as P

D = 2048
HD = 128
TOP = 6
HIGHEST = lax.Precision.HIGHEST


def carried_in(x, axis, join, neutral):
    place = lax.axis_index(axis)
    gathered = lax.all_gather(x.astype(jnp.bfloat16), axis)
    state = jnp.zeros_like(x) + jnp.asarray(neutral, x.dtype)

    def one(turn, state):
        return join(state, lax.dynamic_index_in_dim(gathered, turn, 0, False).astype(x.dtype))

    return lax.fori_loop(0, place, one, state)


def add_states(earlier, later):
    return earlier + later


def shards(
    query_proj,
    key_proj,
    value_proj,
    init_state,
    residual,
    out_gain,
    proj_weight,
    moe_gain,
    w_gate,
    w_up,
    w_down,
    expert_ids,
    gate_weights,
):
    tok_count = query_proj.shape[1]
    feat_width = query_proj.shape[2]
    head_count = feat_width // HD

    def to_heads(matrix):
        return matrix[0].astype(jnp.float32).reshape(tok_count, head_count, HD).transpose(1, 0, 2)

    query_heads = to_heads(query_proj)
    key_heads = to_heads(key_proj)
    value_heads = to_heads(value_proj)
    local_state = jnp.einsum("hsd,hse->hde", key_heads, value_heads, precision=HIGHEST)
    scanned = carried_in(local_state, "seq", add_states, jnp.zeros_like(local_state))
    prior_state = init_state[0] + scanned
    causal = jnp.tril(jnp.ones((tok_count, tok_count), jnp.float32))
    scores = jnp.einsum("htd,hsd->hts", query_heads, key_heads, precision=HIGHEST) * causal
    attended = jnp.einsum("hts,hsd->htd", scores, value_heads, precision=HIGHEST)
    attended = attended + jnp.einsum("htd,hde->hte", query_heads, prior_state, precision=HIGHEST)
    inv_norm = lax.rsqrt(jnp.mean(attended * attended, axis=-1, keepdims=True) + 1e-05)
    mixed = (
        (attended * inv_norm).transpose(1, 0, 2).reshape(tok_count, feat_width) * out_gain
    ).astype(jnp.bfloat16)
    row_count = residual.shape[1]
    wo_full, gate_full, up_full, down_full = (
        lax.all_gather(proj_weight, "expert", axis=1, tiled=True),
        lax.all_gather(w_gate, "expert", axis=2, tiled=True),
        lax.all_gather(w_up, "expert", axis=2, tiled=True),
        lax.all_gather(w_down, "expert", axis=2, tiled=True),
    )
    projected = lax.psum_scatter(
        jnp.dot(mixed, wo_full, preferred_element_type=jnp.float32).astype(jnp.bfloat16),
        "head",
        scatter_dimension=0,
        tiled=True,
    ).astype(jnp.float32)
    stream = (residual[0].astype(jnp.float32) + projected).astype(jnp.bfloat16)
    stream_f = lax.optimization_barrier(stream).astype(jnp.float32)
    moe_in = (
        stream_f
        * lax.rsqrt(jnp.mean(stream_f * stream_f, axis=-1, keepdims=True) + 1e-06)
        * moe_gain
    ).astype(jnp.bfloat16)
    experts_all = w_gate.shape[0] * lax.axis_size(("seq", "head"))
    capacity = max(2, 4 * row_count * TOP // (3 * experts_all))
    chosen = expert_ids[0].reshape(-1)
    onehot = (chosen[:, None] == lax.broadcasted_iota(jnp.int32, (1, experts_all), 1)).astype(
        jnp.int32
    )
    position = jnp.sum((jnp.cumsum(onehot, axis=0) - 1) * onehot, axis=1)
    target = (chosen * capacity + position).reshape(row_count, TOP)
    slot_ids = lax.broadcasted_iota(jnp.int32, (experts_all * capacity, 1, 1), 0)
    placing = jnp.any(target[None, :, :] == slot_ids, axis=-1).astype(jnp.bfloat16)
    outgoing = jnp.dot(placing, moe_in, preferred_element_type=jnp.float32).astype(jnp.bfloat16)
    outgoing = outgoing.reshape(experts_all, capacity, D)
    incoming = lax.all_to_all(outgoing, ("seq", "head"), split_axis=0, concat_axis=1, tiled=True)
    gate_act = jnp.einsum("ehd,erd->ehr", gate_full, incoming, preferred_element_type=jnp.float32)
    up_act = jnp.einsum("ehd,erd->ehr", up_full, incoming, preferred_element_type=jnp.float32)
    hidden = (jax.nn.silu(gate_act) * up_act).astype(jnp.bfloat16)
    results = jnp.einsum(
        "ehr,ehd->erd", hidden, down_full, preferred_element_type=jnp.float32
    ).astype(jnp.bfloat16)
    returned = lax.all_to_all(results, ("seq", "head"), split_axis=1, concat_axis=0, tiled=True)
    gathered_rows = jnp.take(
        returned.reshape(experts_all * capacity, D), target.reshape(-1), axis=0
    )
    gathered_rows = gathered_rows.reshape(row_count, TOP, D)
    combined = jnp.sum(gate_weights[0][:, :, None] * gathered_rows.astype(jnp.float32), axis=1)
    return (stream_f + combined).astype(jnp.bfloat16)[None]


def solution(mesh):
    placed = (
        P("expert", "seq", "head"),
        P("expert", "seq", "head"),
        P("expert", "seq", "head"),
        P("expert", "head", None, None),
        P("expert", ("seq", "head"), None),
        P("head"),
        P("head", "expert"),
        P(),
        P(("seq", "head"), None, "expert"),
        P(("seq", "head"), None, "expert"),
        P(("seq", "head"), None, "expert"),
        P("expert", ("seq", "head"), None),
        P("expert", ("seq", "head"), None),
    )
    return jax.shard_map(
        shards,
        mesh=mesh,
        in_specs=placed,
        out_specs=P("expert", ("seq", "head"), None),
        check_vma=False,
    )
```

profile of v0, /device:TPU:2, one launch (start us, length us, event | category | flops | bytes accessed | tf_op | source)
XLA Modules:
  0.0 490.9 jit_solution(9989508836682642384)
XLA Ops:
  6.5 1.0 copy.95
  7.6 1.1 copy.88
  8.7 0.9 convolution_convert_fusion.3
  9.7 0.7 all-gather.7.cloned.1.call-update
  10.8 106.6 %all-gather.15.cloned.1.call-done = bf16[256,128,128]{2,1,0:T(8,128)(2,1)} async-done(((bf16[8,128,128]{2,1,0:T(8,128)(2,1)}), bf16[256,128,128]{2,1,0:T(8,128)(2,1)}) %all-gather.15.cloned.1.call-update) | async-done | bytes 8388624 | tf_op jit(solution)/shard_map/all_gather | solution.py:14
  117.5 1.2 while.10
  117.5 1.1 convert_add_fusion.4
  119.2 0.7 fusion.44
  120.3 63.5 %all-gather.7.cloned.1.call-done = bf16[1024,2048]{1,0:T(8,128)(2,1)} async-done(((bf16[1024,256]{1,0:T(8,128)(2,1)}), bf16[1024,2048]{1,0:T(8,128)(2,1)}) %all-gather.7.cloned.1.call-update) | async-done | bytes 4194320 | tf_op jit(solution)/shard_map/all_gather | solution.py:65
  183.8 3.8 convolution_convert_fusion.2
  189.7 0.9 reduce-window.6
  191.4 10.7 %reduce-scatter.2.cloned.1.call-done = bf16[64,2048]{1,0:T(8,128)(2,1)} async-done(((bf16[128,2048]{1,0:T(8,128)(2,1)}), bf16[64,2048]{1,0:T(8,128)(2,1)}) %reduce-scatter.2.cloned.1.call-update) | async-done | bytes 262160 | tf_op jit(solution)/shard_map/reduce_scatter | solution.py:70
  202.1 1.0 fusion.41
  203.3 2.2 fusion.5
  205.4 10.3 %all-to-all-start = ((bf16[64,8,2048]{2,1,0:T(8,128)(2,1)}), bf16[64,8,2048]{2,1,0:T(8,128)(2,1)S(1)}, u32[]{:S(2)}, u32[]{:S(2)}) async-start(bf16[64,8,2048]{2,1,0:T(8,128)(2,1)} %fusion.5), calls=%async_computation.1 | async-start | bytes 4194304 | tf_op jit(solution)/shard_map/all_to_all | solution.py:95
  215.7 45.4 %all-gather.9.cloned.1.call-done = bf16[1,704,2048]{2,1,0:T(8,128)(2,1)} async-done(((bf16[1,704,256]{2,1,0:T(8,128)(2,1)}), bf16[1,704,2048]{2,1,0:T(8,128)(2,1)}) %all-gather.9.cloned.1.call-update) | async-done | bytes 2883600 | tf_op jit(solution)/shard_map/all_gather | solution.py:66
  261.1 5.8 %all-to-all-done = bf16[64,8,2048]{2,1,0:T(8,128)(2,1)S(1)} async-done(((bf16[64,8,2048]{2,1,0:T(8,128)(2,1)}), bf16[64,8,2048]{2,1,0:T(8,128)(2,1)S(1)}, u32[]{:S(2)}, u32[]{:S(2)}) %all-to-all-start) | async-done | bytes 2097184 | tf_op jit(solution)/shard_map/all_to_all | solution.py:95
  267.0 5.4 %fusion.11 = f32[704,512]{1,0:T(8,128)} fusion(bf16[1,704,2048]{2,1,0:T(8,128)(2,1)} %all-gather.9.cloned.1.call-done, bf16[64,8,2048]{2,1,0:T(8,128)(2,1)S(1)} %all-to-all-done), kind=kOutput, calls=%fused_computation.16 | convolution fusion | flops 1476395008 | bytes 6422528 | tf_op jit(solution)/shard_map/ehd,erd->ehr/dot_general | solution.py:96
  272.3 45.2 %all-gather.11.cloned.1.call-done = bf16[1,704,2048]{2,1,0:T(8,128)(2,1)} async-done(((bf16[1,704,256]{2,1,0:T(8,128)(2,1)}), bf16[1,704,2048]{2,1,0:T(8,128)(2,1)}) %all-gather.11.cloned.1.call-update) | async-done | bytes 2883600 | tf_op jit(solution)/shard_map/all_gather | solution.py:67
  317.5 56.4 %all-gather.13.cloned.1.call-done = bf16[1,704,2048]{2,1,0:T(8,128)(2,1)} async-done(((bf16[1,704,256]{2,1,0:T(8,128)(2,1)}), bf16[1,704,2048]{2,1,0:T(8,128)(2,1)}) %all-gather.13.cloned.1.call-update) | async-done | bytes 2883600 | tf_op jit(solution)/shard_map/all_gather | solution.py:68
  374.0 7.2 %fusion.6 = bf16[1,512,2048]{2,1,0:T(8,128)(2,1)S(1)} fusion(bf16[1,704,2048]{2,1,0:T(8,128)(2,1)} %all-gather.13.cloned.1.call-done, bf16[1,704,2048]{2,1,0:T(8,128)(2,1)} %all-gather.11.cloned.1.call-done, bf16[64,8,2048]{2,1,0:T(8,128)(2,1)} %copy-done, f32[704,512]{1,0:T(8,128)} %fusion.11), kind=kOutput, calls=%fused_computation.11 | convolution fusion | flops 2956001280 | bytes 11403264 | tf_op jit(solution)/shard_map/ehr,ehd->erd/dot_general | solution.py:99
  381.1 5.2 %copy.121 = bf16[1,512,2048]{2,0,1:T(2,128)(2,1)} copy(bf16[1,512,2048]{2,1,0:T(8,128)(2,1)S(1)} %fusion.6) | data formatting | bytes 4194304 | tf_op jit(solution)/shard_map/convert_element_type | solution.py:101
  386.8 13.2 %reduce.4 = bf16[512,2048]{1,0:T(8,128)(2,1)S(1)} reduce(bf16[512,1,2048]{2,1,0:T(2,128)(2,1)} %bitcast.140, bf16[]{:T(256)} %broadcast.124), dimensions={1}, to_apply=%bitcast.135.reduce_sub_computation | reduce | bytes 4194306
  400.0 3.3 reshape.176
  403.3 10.4 %all-to-all-start.1 = ((bf16[64,2,8192]{2,1,0:T(2,128)(2,1)}), bf16[64,2,8192]{2,1,0:T(2,128)(2,1)S(1)}, u32[]{:S(2)}, u32[]{:S(2)}) async-start(bf16[64,2,8192]{2,1,0:T(2,128)(2,1)} %reshape.176), calls=%async_computation.2 | async-start | bytes 4194304 | tf_op jit(solution)/shard_map/all_to_all | solution.py:102
  414.4 50.5 %all-to-all-done.1 = bf16[64,2,8192]{2,1,0:T(2,128)(2,1)S(1)} async-done(((bf16[64,2,8192]{2,1,0:T(2,128)(2,1)}), bf16[64,2,8192]{2,1,0:T(2,128)(2,1)S(1)}, u32[]{:S(2)}, u32[]{:S(2)}) %all-to-all-start.1) | async-done | bytes 2097184 | tf_op jit(solution)/shard_map/all_to_all | solution.py:102
  464.9 6.8 %reshape.177 = bf16[512,1,2048]{2,1,0:T(2,128)(2,1)} reshape(bf16[64,2,8192]{2,1,0:T(2,128)(2,1)S(1)} %all-to-all-done.1) | data formatting | bytes 4194304
  471.7 3.5 copy.120
  475.2 3.1 gather_fusion
  478.3 2.5 gather.7
  480.8 2.5 multiply_reduce_fusion
  483.3 0.8 fusion.47
  (58 shorter events, 5.5 us)
Async XLA Ops:
  6.5 3.9 copy-start.3
  6.5 110.9 %all-gather.15.cloned.1.call-start = ((), (), s32[]{:S(2)}) async-start(), calls=%async_computation.8 | async-start | bytes 8650752 | tf_op jit(solution)/shard_map/all_gather | solution.py:14
  9.7 174.1 %all-gather.7.cloned.1.call-start = ((), (), s32[]{:S(2)}) async-start(), calls=%async_computation.3 | async-start | bytes 4718592 | tf_op jit(solution)/shard_map/all_gather | solution.py:65
  10.4 191.7 %reduce-scatter.2.cloned.1.call-start = ((), (), s32[]{:S(2)}) async-start(), calls=%async_computation.4 | async-start | bytes 786432 | tf_op jit(solution)/shard_map/reduce_scatter | solution.py:70
  117.4 1.2 copy-start.1
  119.2 0.8 copy-start.6
  120.3 69.0 %copy-start.4 = (s32[1,64,6]{1,0,2:T(1,128)S(1)}, s32[1,64,6]{1,0,2:T(1,128)}, u32[]{:S(2)}) copy-start(s32[1,64,6]{1,0,2:T(1,128)} %param.26) | copy-start | bytes 4612
  187.5 14.5 %copy-start.2 = (bf16[1,64,2048]{2,1,0:T(8,128)(2,1)S(1)}, bf16[1,64,2048]{2,1,0:T(8,128)(2,1)}, u32[]{:S(2)}) copy-start(bf16[1,64,2048]{2,1,0:T(8,128)(2,1)} %param.19) | copy-start | bytes 786436
  187.5 15.7 %copy-start.5 = (f32[2048]{0:T(1024)S(1)}, f32[2048]{0:T(1024)}, u32[]{:S(2)}) copy-start(f32[2048]{0:T(1024)} %param.22) | copy-start | bytes 24580
  187.5 73.6 %all-gather.9.cloned.1.call-start = ((), (), s32[]{:S(2)}) async-start(), calls=%async_computation.5 | async-start | bytes 3244032 | tf_op jit(solution)/shard_map/all_gather | solution.py:66
  188.1 129.4 %all-gather.11.cloned.1.call-start = ((), (), s32[]{:S(2)}) async-start(), calls=%async_computation.6 | async-start | bytes 3244032 | tf_op jit(solution)/shard_map/all_gather | solution.py:67
  188.7 185.2 %all-gather.13.cloned.1.call-start = ((), (), s32[]{:S(2)}) async-start(), calls=%async_computation.7 | async-start | bytes 3244032 | tf_op jit(solution)/shard_map/all_gather | solution.py:68
  205.4 61.5 %all-to-all-start = ((bf16[64,8,2048]{2,1,0:T(8,128)(2,1)}), bf16[64,8,2048]{2,1,0:T(8,128)(2,1)S(1)}, u32[]{:S(2)}, u32[]{:S(2)}) async-start(bf16[64,8,2048]{2,1,0:T(8,128)(2,1)} %fusion.5), calls=%async_computation.1 | async-start | bytes 4194304 | tf_op jit(solution)/shard_map/all_to_all | solution.py:95
  266.9 5.4 %copy-start = (bf16[64,8,2048]{2,1,0:T(8,128)(2,1)}, bf16[64,8,2048]{2,1,0:T(8,128)(2,1)S(1)}, u32[]{:S(2)}) copy-start(bf16[64,8,2048]{2,1,0:T(8,128)(2,1)S(1)} %all-to-all-done) | copy-start | bytes 6291460
  403.3 11.0 %copy-start.7 = (f32[1,64,6]{1,0,2:T(1,128)S(1)}, f32[1,64,6]{1,0,2:T(1,128)}, u32[]{:S(2)}) copy-start(f32[1,64,6]{1,0,2:T(1,128)} %param.27) | copy-start | bytes 4612
  403.3 61.7 %all-to-all-start.1 = ((bf16[64,2,8192]{2,1,0:T(2,128)(2,1)}), bf16[64,2,8192]{2,1,0:T(2,128)(2,1)S(1)}, u32[]{:S(2)}, u32[]{:S(2)}) async-start(bf16[64,2,8192]{2,1,0:T(2,128)(2,1)} %reshape.176), calls=%async_computation.2 | async-start | bytes 4194304 | tf_op jit(solution)/shard_map/all_to_all | solution.py:102
Sparse Core Ops, SparseCore 0:
  10.5 106.8 all-gather.14
  119.4 64.3 all-gather.6
  187.7 14.3 reduce-scatter.1
  204.1 56.9 all-gather.8
  263.2 54.3 all-gather.10
  319.6 54.3 all-gather.12
where the time goes:
time: 492 us; the launch traced here: 491 us
  waiting for transfers between devices  387 us (79%)
  local copies, waits for them, and re-layouts  28.5 us (6%)
  starting transfers between devices  20.9 us (4%)
  matrix products  20.9 us (4%)
  other arithmetic  20.3 us (4%)
  between operations  13.7 us (3%)
    all_gather x1, waiting for transfers between devices, carried_in(): gathered = lax.all_gather(x.astype(jnp.bfloat16), axis)  107 us
    all_gather x1, waiting for transfers between devices, shards(): lax.all_gather(proj_weight, 'expert', axis=1, tiled=True)  63.5 us
    all_gather x1, waiting for transfers between devices, shards(): lax.all_gather(w_down, 'expert', axis=2, tiled=True)  56.4 us
    all_to_all x1, waiting for transfers between devices, shards(): lax.all_to_all(results, ('seq', 'head'), split_axis=1, concat_axis=0, til...  50.5 us
    all_gather x1, waiting for transfers between devices, shards(): lax.all_gather(w_gate, 'expert', axis=2, tiled=True)  45.4 us
    all_gather x1, waiting for transfers between devices, shards(): lax.all_gather(w_up, 'expert', axis=2, tiled=True)  45.2 us
    unnamed x23, local copies, waits for them, and re-layouts  15.2 us
    unnamed x1, other arithmetic  13.2 us
  transfers between devices with their start and end apart: 8, of which 8 were waited for; matrix products, arithmetic and copies ran while one was open for 3% of the time, Pallas kernels for 0%

commit v1 on v0

--- a/solution.py
+++ b/solution.py
@@ -65,7 +65,9 @@
         lax.all_gather(proj_weight, "expert", axis=1, tiled=True),
         lax.all_gather(w_gate, "expert", axis=2, tiled=True),
         lax.all_gather(w_up, "expert", axis=2, tiled=True),
-        lax.all_gather(w_down, "expert", axis=2, tiled=True),
+        jnp.concatenate(
+            lax.all_to_all(jnp.stack([w_down] * lax.axis_size("expert")), "expert", 0, 0), axis=2
+        ),
     )
     projected = lax.psum_scatter(
         jnp.dot(mixed, wo_full, preferred_element_type=jnp.float32).astype(jnp.bfloat16),

time: 492 us -> 468 us (0.951)
  waiting for transfers between devices: 387 us -> 352 us
  local copies, waits for them, and re-layouts: 28.5 us -> 33.9 us
    all_to_all x0 -> x1, waiting for transfers between devices: none -> 67.3 us  [shards(): lax.all_to_all(jnp.stack([w_down] * lax.axis_size('expert')), 'expert', 0...]
    all_gather x1 -> x0, waiting for transfers between devices: 56.4 us -> none  [shards(): lax.all_gather(w_down, 'expert', axis=2, tiled=True)]
    all_gather x1, waiting for transfers between devices: 45.4 us -> 5.42 us  [shards(): lax.all_gather(w_gate, 'expert', axis=2, tiled=True)]
    all_to_all x1, waiting for transfers between devices: 5.83 us -> 43.8 us  [shards(): lax.all_to_all(outgoing, ('seq', 'head'), split_axis=0, concat_axis=1, ti...]
    all_gather x1, waiting for transfers between devices: 45.2 us -> 7.99 us  [shards(): lax.all_gather(w_up, 'expert', axis=2, tiled=True)]
    reduce_scatter x1, waiting for transfers between devices: 10.7 us -> 4.94 us  [shards(): lax.psum_scatter(jnp.dot(mixed, wo_full, preferred_element_type=jnp.float...]
    unnamed x23 -> x26, local copies, waits for them, and re-layouts: 15.2 us -> 17.2 us
  transfers between devices with their start and end apart: 8 -> 8, of which waited for: 8 -> 8; matrix products, arithmetic and copies ran while one was open for 3% -> 4% of each run, Pallas kernels for 0% -> 0%
where the time goes in v1:
time: 468 us; the launch traced here: 466 us
  waiting for transfers between devices  352 us (75%)
  local copies, waits for them, and re-layouts  33.9 us (7%)
  starting transfers between devices  25.5 us (5%)
  matrix products  21.2 us (5%)
  other arithmetic  20.3 us (4%)
  between operations  13.4 us (3%)
    all_gather x1, waiting for transfers between devices, carried_in(): gathered = lax.all_gather(x.astype(jnp.bfloat16), axis)  107 us
    all_to_all x1, waiting for transfers between devices, shards(): lax.all_to_all(jnp.stack([w_down] * lax.axis_size('expert')), 'expert', 0...  67.3 us
    all_gather x1, waiting for transfers between devices, shards(): lax.all_gather(proj_weight, 'expert', axis=1, tiled=True)  63.5 us
    all_to_all x1, waiting for transfers between devices, shards(): lax.all_to_all(results, ('seq', 'head'), split_axis=1, concat_axis=0, til...  50.5 us
    all_to_all x1, waiting for transfers between devices, shards(): lax.all_to_all(outgoing, ('seq', 'head'), split_axis=0, concat_axis=1, ti...  43.8 us
    unnamed x26, local copies, waits for them, and re-layouts  17.2 us
    unnamed x1, other arithmetic  13.2 us
    all_to_all x1, starting transfers between devices, shards(): lax.all_to_all(results, ('seq', 'head'), split_axis=1, concat_axis=0, til...  10.4 us
  transfers between devices with their start and end apart: 8, of which 8 were waited for; matrix products, arithmetic and copies ran while one was open for 4% of the time, Pallas kernels for 0%

profile of v1, /device:TPU:2, one launch (start us, length us, event | category | flops | bytes accessed | tf_op | source)
XLA Modules:
  0.0 466.2 jit_solution(14239424978762427852)
XLA Ops:
  6.5 1.0 copy.99
  7.6 1.1 copy.92
  8.7 0.9 convolution_convert_fusion.3
  10.8 106.6 %all-gather.12.cloned.1.call-done = bf16[256,128,128]{2,1,0:T(8,128)(2,1)} async-done(((bf16[8,128,128]{2,1,0:T(8,128)(2,1)}), bf16[256,128,128]{2,1,0:T(8,128)(2,1)}) %all-gather.12.cloned.1.call-update) | async-done | bytes 8388624 | tf_op jit(solution)/shard_map/all_gather | solution.py:14
  117.5 1.2 while.10
  117.5 1.1 convert_add_fusion.4
  120.3 63.5 %all-gather.6.cloned.1.call-done = bf16[1024,2048]{1,0:T(8,128)(2,1)} async-done(((bf16[1024,256]{1,0:T(8,128)(2,1)}), bf16[1024,2048]{1,0:T(8,128)(2,1)}) %all-gather.6.cloned.1.call-update) | async-done | bytes 4194320 | tf_op jit(solution)/shard_map/all_gather | solution.py:65
  183.8 3.8 convolution_convert_fusion.2
  188.1 1.8 stack.2
  189.9 4.5 all-to-all-start.1
  195.4 0.9 reduce-window.6
  197.1 4.9 %reduce-scatter.2.cloned.1.call-done = bf16[64,2048]{1,0:T(8,128)(2,1)} async-done(((bf16[128,2048]{1,0:T(8,128)(2,1)}), bf16[64,2048]{1,0:T(8,128)(2,1)}) %reduce-scatter.2.cloned.1.call-update) | async-done | bytes 262160 | tf_op jit(solution)/shard_map/reduce_scatter | solution.py:72
  202.1 1.0 fusion.38
  203.3 2.1 fusion.4
  205.4 67.3 %all-to-all-done.1 = bf16[8,1,704,256]{3,2,1,0:T(8,128)(2,1)S(1)} async-done(((bf16[8,1,704,256]{3,2,1,0:T(8,128)(2,1)}), bf16[8,1,704,256]{3,2,1,0:T(8,128)(2,1)S(1)}, u32[]{:S(2)}, u32[]{:S(2)}) %all-to-all-start.1) | async-done | bytes 2883616 | tf_op jit(solution)/shard_map/all_to_all | solution.py:69
  272.7 10.4 %all-to-all-start = ((bf16[64,8,2048]{2,1,0:T(8,128)(2,1)}), bf16[64,8,2048]{2,1,0:T(8,128)(2,1)}, u32[]{:S(2)}, u32[]{:S(2)}) async-start(bf16[64,8,2048]{2,1,0:T(8,128)(2,1)} %fusion.4), calls=%async_computation.1 | async-start | bytes 4194304 | tf_op jit(solution)/shard_map/all_to_all | solution.py:97
  283.1 2.0 copy.100
  285.1 5.4 %all-gather.8.cloned.1.call-done = bf16[1,704,2048]{2,1,0:T(8,128)(2,1)} async-done(((bf16[1,704,256]{2,1,0:T(8,128)(2,1)}), bf16[1,704,2048]{2,1,0:T(8,128)(2,1)}) %all-gather.8.cloned.1.call-update) | async-done | bytes 2883600 | tf_op jit(solution)/shard_map/all_gather | solution.py:66
  290.5 43.8 %all-to-all-done = bf16[64,8,2048]{2,1,0:T(8,128)(2,1)} async-done(((bf16[64,8,2048]{2,1,0:T(8,128)(2,1)}), bf16[64,8,2048]{2,1,0:T(8,128)(2,1)}, u32[]{:S(2)}, u32[]{:S(2)}) %all-to-all-start) | async-done | bytes 2097184 | tf_op jit(solution)/shard_map/all_to_all | solution.py:97
  334.3 5.3 %fusion.8 = f32[704,512]{1,0:T(8,128)} fusion(bf16[1,704,2048]{2,1,0:T(8,128)(2,1)} %all-gather.8.cloned.1.call-done, bf16[64,8,2048]{2,1,0:T(8,128)(2,1)} %all-to-all-done), kind=kOutput, calls=%fused_computation.15 | convolution fusion | flops 1476395008 | bytes 6422528 | tf_op jit(solution)/shard_map/ehd,erd->ehr/dot_general | solution.py:98
  339.5 8.0 %all-gather.10.cloned.1.call-done = bf16[1,704,2048]{2,1,0:T(8,128)(2,1)} async-done(((bf16[1,704,256]{2,1,0:T(8,128)(2,1)}), bf16[1,704,2048]{2,1,0:T(8,128)(2,1)}) %all-gather.10.cloned.1.call-update) | async-done | bytes 2883600 | tf_op jit(solution)/shard_map/all_gather | solution.py:67
  347.5 7.6 %fusion.5 = bf16[1,512,2048]{2,1,0:T(8,128)(2,1)} fusion(bf16[704,2048]{1,0:T(8,128)(2,1)S(1)} %bitcast.146, bf16[1,704,2048]{2,1,0:T(8,128)(2,1)} %all-gather.10.cloned.1.call-done, bf16[64,8,2048]{2,1,0:T(8,128)(2,1)} %all-to-all-done, f32[704,512]{1,0:T(8,128)} %fusion.8), kind=kOutput, calls=%fused_computation.10 | convolution fusion | flops 2956001280 | bytes 11403264 | tf_op jit(solution)/shard_map/ehr,ehd->erd/dot_general | solution.py:101
  355.2 6.8 %copy.127 = bf16[1,512,2048]{2,0,1:T(2,128)(2,1)} copy(bf16[1,512,2048]{2,1,0:T(8,128)(2,1)} %fusion.5) | data formatting | bytes 4194304 | tf_op jit(solution)/shard_map/convert_element_type | solution.py:103
  362.5 13.2 %reduce.4 = bf16[512,2048]{1,0:T(8,128)(2,1)S(1)} reduce(bf16[512,1,2048]{2,1,0:T(2,128)(2,1)} %bitcast.143, bf16[]{:T(256)} %broadcast.127), dimensions={1}, to_apply=%bitcast.138.reduce_sub_computation | reduce | bytes 4194306
  375.6 3.3 reshape.185
  378.9 10.4 %all-to-all-start.2 = ((bf16[64,2,8192]{2,1,0:T(2,128)(2,1)}), bf16[64,2,8192]{2,1,0:T(2,128)(2,1)S(1)}, u32[]{:S(2)}, u32[]{:S(2)}) async-start(bf16[64,2,8192]{2,1,0:T(2,128)(2,1)} %reshape.185), calls=%async_computation.3 | async-start | bytes 4194304 | tf_op jit(solution)/shard_map/all_to_all | solution.py:104
  390.0 50.5 %all-to-all-done.2 = bf16[64,2,8192]{2,1,0:T(2,128)(2,1)S(1)} async-done(((bf16[64,2,8192]{2,1,0:T(2,128)(2,1)}), bf16[64,2,8192]{2,1,0:T(2,128)(2,1)S(1)}, u32[]{:S(2)}, u32[]{:S(2)}) %all-to-all-start.2) | async-done | bytes 2097184 | tf_op jit(solution)/shard_map/all_to_all | solution.py:104
  440.6 6.8 %reshape.186 = bf16[512,1,2048]{2,1,0:T(2,128)(2,1)} reshape(bf16[64,2,8192]{2,1,0:T(2,128)(2,1)S(1)} %all-to-all-done.2) | data formatting | bytes 4194304
  447.3 3.5 copy.126
  450.8 3.1 gather_fusion
  453.9 2.5 gather.7
  456.4 2.5 multiply_reduce_fusion
  (61 shorter events, 7.2 us)
Async XLA Ops:
  6.5 3.9 copy-start.4
  6.5 110.9 %all-gather.12.cloned.1.call-start = ((), (), s32[]{:S(2)}) async-start(), calls=%async_computation.8 | async-start | bytes 8650752 | tf_op jit(solution)/shard_map/all_gather | solution.py:14
  9.7 174.1 %all-gather.6.cloned.1.call-start = ((), (), s32[]{:S(2)}) async-start(), calls=%async_computation.4 | async-start | bytes 4718592 | tf_op jit(solution)/shard_map/all_gather | solution.py:65
  10.4 191.6 %reduce-scatter.2.cloned.1.call-start = ((), (), s32[]{:S(2)}) async-start(), calls=%async_computation.5 | async-start | bytes 786432 | tf_op jit(solution)/shard_map/reduce_scatter | solution.py:72
  117.4 1.2 copy-start.1
  119.2 0.8 copy-start.7
  120.3 67.9 %copy-start.2 = (bf16[1,704,256]{2,1,0:T(8,128)(2,1)S(1)}, bf16[1,704,256]{2,1,0:T(8,128)(2,1)}, u32[]{:S(2)}) copy-start(bf16[1,704,256]{2,1,0:T(8,128)(2,1)} %param.25) | copy-start | bytes 1081348
  187.5 103.0 %all-gather.8.cloned.1.call-start = ((), (), s32[]{:S(2)}) async-start(), calls=%async_computation.6 | async-start | bytes 3244032 | tf_op jit(solution)/shard_map/all_gather | solution.py:66
  189.9 5.1 %copy-start.5 = (s32[1,64,6]{1,0,2:T(1,128)S(1)}, s32[1,64,6]{1,0,2:T(1,128)}, u32[]{:S(2)}) copy-start(s32[1,64,6]{1,0,2:T(1,128)} %param.26) | copy-start | bytes 4612
  189.9 12.2 %copy-start.3 = (bf16[1,64,2048]{2,1,0:T(8,128)(2,1)S(1)}, bf16[1,64,2048]{2,1,0:T(8,128)(2,1)}, u32[]{:S(2)}) copy-start(bf16[1,64,2048]{2,1,0:T(8,128)(2,1)} %param.19) | copy-start | bytes 786436
  189.9 82.8 %all-to-all-start.1 = ((bf16[8,1,704,256]{3,2,1,0:T(8,128)(2,1)}), bf16[8,1,704,256]{3,2,1,0:T(8,128)(2,1)S(1)}, u32[]{:S(2)}, u32[]{:S(2)}) async-start(bf16[8,1,704,256]{3,2,1,0:T(8,128)(2,1)} %stack.2), calls=%async_computation.2 | async-start | bytes 5767168 | tf_op jit(solution)/shard_map/all_to_all | solution.py:69
  194.4 8.8 %copy-start.6 = (f32[2048]{0:T(1024)S(1)}, f32[2048]{0:T(1024)}, u32[]{:S(2)}) copy-start(f32[2048]{0:T(1024)} %param.22) | copy-start | bytes 24580
  194.4 153.1 %all-gather.10.cloned.1.call-start = ((), (), s32[]{:S(2)}) async-start(), calls=%async_computation.7 | async-start | bytes 3244032 | tf_op jit(solution)/shard_map/all_gather | solution.py:67
  272.7 61.6 %all-to-all-start = ((bf16[64,8,2048]{2,1,0:T(8,128)(2,1)}), bf16[64,8,2048]{2,1,0:T(8,128)(2,1)}, u32[]{:S(2)}, u32[]{:S(2)}) async-start(bf16[64,8,2048]{2,1,0:T(8,128)(2,1)} %fusion.4), calls=%async_computation.1 | async-start | bytes 4194304 | tf_op jit(solution)/shard_map/all_to_all | solution.py:97
  285.1 62.4 %copy-start = (bf16[88,8,8,256]{3,1,2,0:T(8,128)(2,1)S(1)}, bf16[88,8,8,256]{3,1,2,0:T(8,128)(2,1)}, u32[]{:S(2)}) copy-start(bf16[88,8,8,256]{3,1,2,0:T(8,128)(2,1)} %copy.100) | copy-start | bytes 8650756
  378.9 11.0 %copy-start.8 = (f32[1,64,6]{1,0,2:T(1,128)S(1)}, f32[1,64,6]{1,0,2:T(1,128)}, u32[]{:S(2)}) copy-start(f32[1,64,6]{1,0,2:T(1,128)} %param.27) | copy-start | bytes 4612
  378.9 61.7 %all-to-all-start.2 = ((bf16[64,2,8192]{2,1,0:T(2,128)(2,1)}), bf16[64,2,8192]{2,1,0:T(2,128)(2,1)S(1)}, u32[]{:S(2)}, u32[]{:S(2)}) async-start(bf16[64,2,8192]{2,1,0:T(2,128)(2,1)} %reshape.185), calls=%async_computation.3 | async-start | bytes 4194304 | tf_op jit(solution)/shard_map/all_to_all | solution.py:104
Sparse Core Ops, SparseCore 0:
  10.5 106.8 all-gather.11
  119.4 64.3 all-gather.5
  187.7 14.3 reduce-scatter.1
  204.1 86.3 all-gather.7
  292.6 54.9 all-gather.9
